TPU v7x, 32 devices: a whole 2x2x4 slice. The times are simulated.
32 devices in a mesh: groups: 1, vocab: 4 (over z), tokens: 4 (over y, x), sub: 2 (over core).
Axes of the slice: x: 2, y: 2, z: 4, core: 2. Of those that a mesh axis runs over, the one named last changes fastest.
Arguments:
- student_hidden: bfloat16 [32, 3072], P(('groups', 'vocab', 'tokens', 'sub')), may hold values from -41 to 41
- teacher_hidden: bfloat16 [32, 4096], P(('groups', 'vocab', 'tokens', 'sub')), may hold values from -41 to 41
- student_head: bfloat16 [3072, 8192], P(None, ('vocab', 'tokens', 'sub')), may hold values from -0.25 to 0.25
- teacher_head: bfloat16 [4096, 8192], P(None, ('vocab', 'tokens', 'sub')), may hold values from -0.1875 to 0.1875
- proposed_block: int32 [32, 32], P(('groups', 'vocab', 'tokens', 'sub')), may hold values from 0 to 63, all different within a row; in each aligned block of 32 rows (0 to 31, 32 to 63, ...) at most 32 rows name the same one
- proposed_offset: int32 [32, 32], P(('groups', 'vocab', 'tokens', 'sub')), may hold values from 0 to 127
Outputs:
- token_loss: float32 [32], P(('groups', 'vocab', 'tokens', 'sub'))
- student_grad: bfloat16 [32, 3072], P(('groups', 'vocab', 'tokens', 'sub'))
Inputs may be any that keep to these rules, and one draw needn't show every extreme that they name: `proposed_block`: each token names 32 different blocks; within one replica no block is named by more than 32 tokens, and some block by exactly 32.
All inputs are finite; a program needn't handle non-finite values.
Results may differ from a plain program's by a relative error of at most 0.014.
Values may be sent and summed in bfloat16 or wider, within the bound.
A program may use at most 64 MiB of HBM per device.

v0:
```python
import math

import jax
import jax.numpy as jnp
from jax import lax
from jax.sharding import PartitionSpec as P

BLK = 128


mix_weight = 0.1
loss_scale = 64.0


def loss_terms(student_at, teacher_at, student_norm, teacher_norm):
    student_logprob = student_at - student_norm[:, None]
    teacher_logprob = teacher_at - teacher_norm[:, None]
    shifted = jnp.exp(student_at - jnp.max(student_at, axis=1, keepdims=True))
    weights = shifted / jnp.sum(shifted, axis=1, keepdims=True)
    mixture = jnp.logaddexp(
        student_logprob + math.log(mix_weight), teacher_logprob + math.log(1.0 - mix_weight)
    )
    excess = student_logprob - mixture
    token_loss = jnp.sum(weights * excess, axis=1)
    mix_share = jnp.exp(student_logprob + math.log(mix_weight) - mixture)
    direct = weights * (1.0 - mix_share)
    grad_at = loss_scale * (weights * (excess - token_loss[:, None]) + direct)
    grad_mass = loss_scale * jnp.sum(direct, axis=1)
    return (token_loss, grad_at, grad_mass)


def local(
    student_hidden, teacher_hidden, student_head, teacher_head, proposed_block, proposed_offset
):
    tok_dev = student_hidden.shape[0]
    col_width = student_head.shape[1]
    shards = lax.axis_size(("vocab", "tokens", "sub"))
    shard_index = lax.axis_index(("vocab", "tokens", "sub"))
    tokens = tok_dev * shards
    blocks_here = col_width // BLK
    token_iota = jnp.arange(tokens, dtype=jnp.int32)
    block_all, offset_all = (
        lax.all_gather(proposed_block, ("vocab", "tokens", "sub"), axis=0, tiled=True),
        lax.all_gather(proposed_offset, ("vocab", "tokens", "sub"), axis=0, tiled=True),
    )
    local_ids = block_all * BLK + offset_all - shard_index * col_width
    is_owned = (local_ids >= 0) & (local_ids < col_width)
    local_col = jnp.clip(local_ids, 0, col_width - 1)
    block_here = block_all - shard_index * blocks_here
    touched = jnp.any(
        block_here[:, :, None] == jnp.arange(blocks_here, dtype=jnp.int32)[None, None, :], axis=1
    )
    student_all = lax.all_gather(student_hidden, ("vocab", "tokens", "sub"), axis=0, tiled=True)
    student_logits = jnp.dot(student_all, student_head, preferred_element_type=jnp.float32)
    student_peak = jnp.max(student_logits, axis=1)
    student_at = jnp.where(is_owned, jnp.take_along_axis(student_logits, local_col, axis=1), 0.0)
    teacher_all = lax.all_gather(teacher_hidden, ("vocab", "tokens", "sub"), axis=0, tiled=True)
    col_mask = jnp.repeat(touched, BLK, axis=1)
    teacher_logits = jnp.dot(teacher_all, teacher_head, preferred_element_type=jnp.float32)
    teacher_peak = jnp.max(jnp.where(col_mask, teacher_logits, -1e30), axis=1)
    teacher_at = jnp.where(is_owned, jnp.take_along_axis(teacher_logits, local_col, axis=1), 0.0)
    student_peak, teacher_peak = lax.pmax((student_peak, teacher_peak), ("vocab", "tokens", "sub"))
    student_total, teacher_total, student_at, teacher_at = lax.psum(
        (
            jnp.sum(jnp.exp(student_logits - student_peak[:, None]), axis=1),
            jnp.sum(
                jnp.exp(jnp.where(col_mask, teacher_logits - teacher_peak[:, None], -1e30)), axis=1
            ),
            student_at,
            teacher_at,
        ),
        ("vocab", "tokens", "sub"),
    )
    student_norm = student_peak + jnp.log(student_total)
    teacher_norm = teacher_peak + jnp.log(teacher_total)
    token_loss, grad_at, grad_mass = loss_terms(student_at, teacher_at, student_norm, teacher_norm)
    loss_here = lax.dynamic_slice_in_dim(token_loss, shard_index * tok_dev, tok_dev)
    logit_grad = -grad_mass[:, None] * jnp.exp(student_logits - student_norm[:, None])
    logit_grad = logit_grad.at[token_iota[:, None], local_col].add(
        jnp.where(is_owned, grad_at, 0.0)
    )
    grad_narrow = logit_grad.astype(jnp.bfloat16)
    partial_value = lax.psum_scatter(
        lax.dot_general(
            grad_narrow, student_head, (((1,), (1,)), ((), ())), preferred_element_type=jnp.float32
        ).astype(jnp.bfloat16),
        "vocab",
        scatter_dimension=0,
        tiled=True,
    )
    grad_here = lax.psum_scatter(
        partial_value, ("tokens", "sub"), scatter_dimension=0, tiled=True
    ).astype(jnp.float32)
    return (loss_here, grad_here.astype(jnp.bfloat16))


def solution(mesh):
    return jax.shard_map(
        local,
        mesh=mesh,
        in_specs=(
            P(("groups", "vocab", "tokens", "sub"), None),
            P(("groups", "vocab", "tokens", "sub"), None),
            P(None, ("vocab", "tokens", "sub")),
            P(None, ("vocab", "tokens", "sub")),
            P(("groups", "vocab", "tokens", "sub"), None),
            P(("groups", "vocab", "tokens", "sub"), None),
        ),
        out_specs=(
            P(("groups", "vocab", "tokens", "sub")),
            P(("groups", "vocab", "tokens", "sub"), None),
        ),
        check_vma=False,
    )
```

profile of v0, /device:TPU:0, one launch (start us, length us, event | category | flops | bytes accessed | tf_op | source)
XLA Modules:
  0.0 326.5 jit_solution(7705436805883935377)
XLA Ops:
  7.2 43.3 %all-gather = s32[32,1,32]{2,1,0:T(1,128)S(1)} all-gather(s32[1,1,32]{2,1,0:T(1,128)} %bitcast.62), channel_id=1, replica_groups=mesh['groups'=1,'vocab'=4,'tokens'=4,'sub'=2] {'vocab','tokens','sub'}, dimensions={0}, use_global_device_ids=true | all-gather | bytes 4224 | tf_op jit(solution)/shard_map/all_gather | solution.py:43
  50.6 0.1 fusion.6
  50.8 38.3 %all-gather.3 = bf16[32,1,4096]{2,1,0:T(2,128)(2,1)S(1)} all-gather(bf16[1,1,4096]{2,1,0:T(2,128)(2,1)} %bitcast.60), channel_id=1, replica_groups=mesh['groups'=1,'vocab'=4,'tokens'=4,'sub'=2] {'vocab','tokens','sub'}, dimensions={0}, use_global_device_ids=true | all-gather | bytes 270336 | tf_op jit(solution)/shard_map/all_gather | solution.py:57
  89.1 38.0 %all-gather.1 = s32[32,1,32]{2,1,0:T(1,128)S(1)} all-gather(s32[1,1,32]{2,1,0:T(1,128)} %bitcast.63), channel_id=1, replica_groups=mesh['groups'=1,'vocab'=4,'tokens'=4,'sub'=2] {'vocab','tokens','sub'}, dimensions={0}, use_global_device_ids=true | all-gather | bytes 4224 | tf_op jit(solution)/shard_map/all_gather | solution.py:44
  127.3 0.6 select_reduce_fusion
  127.9 8.6 %gather_fusion.1 = f32[1024]{0:T(1024)S(1)} fusion(f32[32,256]{1,0:T(8,128)S(1)} %get-tuple-element.17, s32[1024]{0:T(1024)S(1)} %reshape.88), kind=kCustom, calls=%fused_computation.1.clone | custom fusion | bytes 16384 | tf_op jit(solution)/shard_map/jit(take_along_axis)/gather | solution.py:61
  136.6 37.7 %all-gather.2 = bf16[32,1,3072]{2,1,0:T(2,128)(2,1)S(1)} all-gather(bf16[1,1,3072]{2,1,0:T(2,128)(2,1)S(1)} %bitcast.61), channel_id=1, replica_groups=mesh['groups'=1,'vocab'=4,'tokens'=4,'sub'=2] {'vocab','tokens','sub'}, dimensions={0}, use_global_device_ids=true | all-gather | bytes 202752 | tf_op jit(solution)/shard_map/all_gather | solution.py:53
  174.3 1.8 fusion.10
  176.2 8.6 %gather_fusion = f32[1024]{0:T(1024)S(1)} fusion(f32[32,256]{1,0:T(8,128)S(1)} %get-tuple-element.19, s32[1024]{0:T(1024)S(1)} %reshape.88), kind=kCustom, calls=%fused_computation.clone | custom fusion | bytes 16384 | tf_op jit(solution)/shard_map/jit(take_along_axis)/gather | solution.py:56
  184.8 37.0 %all-reduce.2 = (f32[32]{0:T(128)S(1)}, f32[32]{0:T(128)S(1)}) all-reduce(f32[32]{0:T(128)S(1)} %get-tuple-element.16, f32[32]{0:T(128)S(1)} %get-tuple-element.18), channel_id=1, replica_groups=mesh['groups'=1,'vocab'=4,'tokens'=4,'sub'=2] {'vocab','tokens','sub'}, use_global_device_ids=true, to_apply=%region_10.12 | all-reduce | flops 64 | bytes 512 | tf_op jit(solution)/shard_map/pmax | solution.py:62
  221.9 0.2 exponential_reduce_fusion
  222.1 42.9 %all-reduce.1 = (f32[32,32]{1,0:T(8,128)S(1)}, f32[32,32]{1,0:T(8,128)S(1)}, f32[32]{0:T(128)S(1)}, f32[32]{0:T(128)S(1)}) all-reduce(f32[32,32]{1,0:T(8,128)S(1)} %select_select_fusion.1, f32[32,32]{1,0:T(8,128)S(1)} %get-tuple-element.13, ...), channel_id=1, replica_groups=mesh['groups'=1,'vocab'=4,'tokens'=4,'sub'=2] {'vocab','tokens','sub'}, use_global_device_ids=true, to_apply=%region_0.0 | all-reduce | flops 2112 | bytes 16896 | tf_op jit(solution)/shard_map/psum | solution.py:63
  265.0 0.1 reduce_max.27
  265.1 0.2 fusion.8
  265.3 0.2 multiply_reduce_fusion.1
  265.5 0.1 multiply_select_fusion
  265.6 0.1 reduce_sum.49
  266.2 7.6 %scatter_fusion = f32[8192]{0:T(1024)S(1)} fusion(f32[8192]{0:T(1024)S(1)} %bitcast.53, s32[1024]{0:T(1024)S(1)} %reshape.49, f32[1024]{0:T(1024)S(1)} %reshape.51), kind=kCustom, calls=%fused_computation.2 | custom fusion | flops 1024 | bytes 16384
  273.9 2.7 convolution_convert_fusion
  276.6 0.6 dynamic_slice.3
  277.2 0.6 dynamic-slice
  277.8 17.3 %reduce-scatter.2.cloned.1.call-done = bf16[8,3072]{1,0:T(8,128)(2,1)} async-done(((bf16[32,3072]{1,0:T(8,128)(2,1)}), bf16[8,3072]{1,0:T(8,128)(2,1)}) %reduce-scatter.2.cloned.1.call-update) | async-done | bytes 49168 | tf_op jit(solution)/shard_map/reduce_scatter | solution.py:83
  295.1 23.3 %all-reduce = bf16[8,3072]{1,0:T(8,128)(2,1)S(1)} all-reduce(bf16[8,3072]{1,0:T(8,128)(2,1)} %reduce-scatter.2.cloned.1.call-done), channel_id=3, replica_groups=mesh['groups'=1,'vocab'=4,'tokens'=4,'sub'=2] {'tokens','sub'}, use_global_device_ids=true, to_apply=%region_17.19.clone | all-reduce | flops 24576 | bytes 98304
  318.4 1.2 constant_dynamic-slice_fusion
  (35 shorter events, 1.0 us)
Async XLA Ops:
  7.2 120.1 %copy-start = (bf16[4096,256]{1,0:T(8,128)(2,1)S(1)}, bf16[4096,256]{1,0:T(8,128)(2,1)}, u32[]{:S(2)}) copy-start(bf16[4096,256]{1,0:T(8,128)(2,1)} %param.11) | copy-start | bytes 6291460
  7.2 287.9 %reduce-scatter.2.cloned.1.call-start = ((), (), s32[]{:S(2)}) async-start(), calls=%async_computation.1 | async-start | bytes 245760 | tf_op jit(solution)/shard_map/reduce_scatter | solution.py:83
  127.9 8.7 %copy-start.1 = (bf16[1,3072]{1,0:T(2,128)(2,1)S(1)}, bf16[1,3072]{1,0:T(2,128)(2,1)}, u32[]{:S(2)}) copy-start(bf16[1,3072]{1,0:T(2,128)(2,1)} %param.8) | copy-start | bytes 18436
  176.1 89.8 %copy-start.3 = (s32[2]{0:T(128)S(1)}, s32[2]{0:T(128)}, u32[]{:S(2)}) copy-start(s32[2]{0:T(128)} %constant.61) | copy-start | bytes 28
  176.1 89.9 %copy-start.2 = (s32[2]{0:T(128)S(1)}, s32[2]{0:T(128)}, u32[]{:S(2)}) copy-start(s32[2]{0:T(128)} %constant.64) | copy-start | bytes 28
  273.9 3.3 %copy-start.4 = (u32[32]{0:T(128)S(1)}, u32[32]{0:T(128)}, u32[]{:S(2)}) copy-start(u32[32]{0:T(128)} %constant.109) | copy-start | bytes 388
Sparse Core Ops, SparseCore 0:
  276.7 18.3 reduce-scatter.1
where the time goes:
time: 327 us
  blocking collectives  261 us (80%)
  local copies, waits for them, and re-layouts  20.3 us (6%)
  waiting for transfers between devices  17.3 us (5%)
  between operations  14.2 us (4%)
  other arithmetic  9.01 us (3%)
  matrix products  5.12 us (2%)
    all_gather x1, blocking collectives, local(): lax.all_gather(proposed_block, ('vocab', 'tokens', 'sub'), axis=0, tiled=...  43.3 us
    psum x1, blocking collectives, local(): lax.psum((jnp.sum(jnp.exp(student_logits - student_peak[:, None]), axis=1...  42.9 us
    all_gather x1, blocking collectives, local(): lax.all_gather(teacher_hidden, ('vocab', 'tokens', 'sub'), axis=0, tiled=...  38.3 us
    all_gather x1, blocking collectives, local(): lax.all_gather(proposed_offset, ('vocab', 'tokens', 'sub'), axis=0, tiled...  38 us
    all_gather x1, blocking collectives, local(): lax.all_gather(student_hidden, ('vocab', 'tokens', 'sub'), axis=0, tiled=...  37.7 us
    pmax x1, blocking collectives, local(): lax.pmax((student_peak, teacher_peak), ('vocab', 'tokens', 'sub'))  37 us
    unnamed x1, blocking collectives  23.3 us
    reduce_scatter x1, waiting for transfers between devices, local(): lax.psum_scatter(lax.dot_general(grad_narrow, student_head, (((1,), (1,))...  17.3 us
  transfers between devices with their start and end apart: 1, of which 1 were waited for; matrix products, arithmetic and copies ran while one was open for 0% of the time, Pallas kernels for 0%

commit v1 on v0

v1 whole, which is shorter than its diff:
```python
import functools
import math

import jax
import jax.numpy as jnp
from jax import lax
from jax.experimental import pallas as pl
from jax.experimental.pallas import tpu as pltpu
from jax.sharding import PartitionSpec as P

BLK = 128
LANES = 128
NONE = -1e30
AXES = ("vocab", "tokens", "sub")
mix_weight = 0.1
loss_scale = 64.0
MESH = pl.DeviceIdType.MESH


def loss_planes(at, student_max, student_sum, teacher_max, teacher_sum):
    top = lambda x: jnp.max(x, axis=0, keepdims=True)
    add = lambda x: jnp.sum(x, axis=0, keepdims=True)
    peak = top(student_max)
    student_norm = peak + jnp.log(add(student_sum * jnp.exp(student_max - peak)))
    teacher_peak = top(teacher_max)
    teacher_norm = teacher_peak + jnp.log(add(teacher_sum * jnp.exp(teacher_max - teacher_peak)))
    at_peak = functools.reduce(jnp.maximum, [top(s) for s, _ in at])
    shifted = [jnp.exp(s - at_peak) for s, _ in at]
    scale = 1.0 / sum(add(x) for x in shifted)
    weights = [x * scale for x in shifted]
    excess, direct = [], []
    for (student, teacher), weight in zip(at, weights):
        a = student - student_norm + math.log(mix_weight)
        b = teacher - teacher_norm + math.log(1.0 - mix_weight)
        mixture = jnp.maximum(a, b) + jnp.log(1.0 + jnp.exp(-jnp.abs(a - b)))
        excess.append(student - student_norm - mixture)
        direct.append(weight * (1.0 - jnp.exp(a - mixture)))
    token_loss = sum(add(w * e) for w, e in zip(weights, excess))
    grad_at = [loss_scale * (w * (e - token_loss) + d) for w, e, d in zip(weights, excess, direct)]
    mass = loss_scale * sum(add(d) for d in direct)
    return token_loss, grad_at, mass, student_norm


def kernel(
    sizes, sh_hbm, th_hbm, ws_hbm, wt_hbm, blk_hbm, off_hbm, loss_ref, grad_ref,
    sh, th, ws, wt, blk, off, stage, gbuf, xs, sbuf, ps, pbuf, rbuf,
    load_sem, gz_sem, gx_sem, gc_sem, gr_sem, ss_sem, sr_sem, ps_sem, pr_sem,
):
    V, T, S = sizes
    n = V * T * S
    g = lax.axis_index("groups")
    v, t, s = (lax.axis_index(a) for a in AXES)
    me = (v * T + t) * S + s
    ds_rows, dt_rows = sh.shape[1] // LANES, th.shape[1] // LANES
    rows = gbuf.shape[1]

    def device(p):
        return (g, p // (T * S), (p // S) % T, p % S)

    def slot(a, b, c):
        return (a * T + b) * S + c

    loads = [
        pltpu.make_async_copy(src, dst, load_sem.at[i])
        for i, (src, dst) in enumerate(
            [(sh_hbm, sh), (th_hbm, th), (blk_hbm, blk), (off_hbm, off), (ws_hbm, ws), (wt_hbm, wt)]
        )
    ]
    for load in loads:
        load.start()

    barrier = pltpu.get_barrier_semaphore()

    @pl.loop(1, n)
    def _(i):
        pl.semaphore_signal(barrier, inc=1, device_id=device(lax.rem(me + i, n)), device_id_type=MESH)

    for load in loads[:4]:
        load.wait()

    for j in range(ds_rows):
        stage[j : j + 1, :] = sh[:, j * LANES : (j + 1) * LANES].astype(jnp.float32)
    for j in range(dt_rows):
        stage[ds_rows + j : ds_rows + j + 1, :] = th[:, j * LANES : (j + 1) * LANES].astype(jnp.float32)
    K = blk.shape[1]
    base = ds_rows + dt_rows
    stage[base : base + 8, :] = jnp.zeros((8, LANES), jnp.float32)
    block_row = blk[...]
    stage[base : base + 1, :K] = (block_row // 64).astype(jnp.float32)
    stage[base + 1 : base + 2, :K] = (block_row % 64).astype(jnp.float32)
    stage[base + 2 : base + 3, :K] = off[...].astype(jnp.float32)
    gbuf[me] = stage[...].astype(jnp.bfloat16)

    pl.semaphore_wait(barrier, n - 1)

    def send(at, to, sem):
        return pltpu.make_async_remote_copy(
            src_ref=gbuf.at[at], dst_ref=gbuf.at[at], send_sem=sem, recv_sem=gr_sem.at[at],
            device_id=to, device_id_type=MESH,
        )

    other = lax.rem(s + 1, S)

    def to_z(d):
        return send(me, (g, lax.rem(v + d, V), t, s), gz_sem.at[d])

    def to_xy(a, d):
        return send(slot(a, t, s), (g, v, lax.rem(t + d, T), s), gx_sem.at[a, d])

    def to_core(a, b):
        return send(slot(a, b, s), (g, v, t, other), gc_sem.at[a, b])

    def unpack(at):
        xs[pl.ds(at, rows, stride=n), :] = gbuf[at].astype(jnp.float32)

    @pl.loop(1, V)
    def _(d):
        to_z(d).start()

    for d in range(1, T):
        to_xy(v, d).start()
    to_core(v, t).start()
    unpack(me)

    @pl.loop(1, V)
    def _(d):
        a = lax.rem(v + V - d, V)
        send(slot(a, t, s), (g, v, t, other), gc_sem.at[a, t]).wait_recv()
        for e in range(1, T):
            to_xy(a, e).start()
        to_core(a, t).start()
        unpack(slot(a, t, s))

    @pl.loop(0, V)
    def _(d):
        a = lax.rem(v + V - d, V)
        for e in range(1, T):
            b = lax.rem(t + T - e, T)
            to_core(a, b).wait_recv()
            to_core(a, b).start()
            unpack(slot(a, b, s))

    @pl.loop(0, V)
    def _(d):
        a = lax.rem(v + V - d, V)
        for e in range(T):
            b = lax.rem(t + T - e, T)
            at = slot(a, b, other)
            send(at, (g, v, t, other), gc_sem.at[a, b]).wait_recv()
            unpack(at)

    def chunks(lo, hi):
        return jnp.concatenate([xs[c * n : (c + 1) * n, :] for c in range(lo, hi)], axis=1).astype(jnp.bfloat16)

    loads[4].wait()
    student = jnp.dot(chunks(0, ds_rows), ws[...], preferred_element_type=jnp.float32)
    loads[5].wait()
    teacher = jnp.dot(chunks(ds_rows, base), wt[...], preferred_element_type=jnp.float32)

    col_width = ws.shape[1]
    here = col_width // BLK
    block_all = xs[base * n : (base + 1) * n, :] * 64.0 + xs[(base + 1) * n : (base + 2) * n, :]
    offset_all = xs[(base + 2) * n : (base + 3) * n, :] + 1.0
    lane = lax.broadcasted_iota(jnp.int32, (n, LANES), 1)
    student_at, teacher_at, hits, masked = [], [], [], []
    for b in range(here):
        wanted = (me * here + b).astype(jnp.float32)
        chosen = jnp.where((block_all == wanted) & (lane < K), offset_all, 0.0)
        offset = jnp.sum(chosen, axis=1, keepdims=True)
        named = offset > 0.0
        hit = lane.astype(jnp.float32) + 1.0 == offset
        part = slice(b * BLK, (b + 1) * BLK)
        at_s = jnp.sum(jnp.where(hit, student[:, part], 0.0), axis=1, keepdims=True)
        student_at.append(jnp.where(named, at_s, NONE))
        teacher_at.append(jnp.sum(jnp.where(hit, teacher[:, part], 0.0), axis=1, keepdims=True))
        hits.append(hit)
        masked.append(jnp.where(named, teacher[:, part], NONE))
    teacher_seen = jnp.concatenate(masked, axis=1)
    student_max = jnp.max(student, axis=1, keepdims=True)
    student_sum = jnp.sum(jnp.exp(student - student_max), axis=1, keepdims=True)
    teacher_max = jnp.max(teacher_seen, axis=1, keepdims=True)
    teacher_sum = jnp.sum(
        jnp.where(teacher_seen > 0.5 * NONE, jnp.exp(teacher_seen - teacher_max), 0.0), axis=1, keepdims=True
    )
    values = student_at + teacher_at + [student_max, student_sum, teacher_max, teacher_sum]

    span = min(n, LANES)
    per = LANES // span
    planes = n // span
    width = len(values) // per
    wide = lax.broadcasted_iota(jnp.int32, (span, LANES), 1)
    for c in range(planes):
        parts = []
        for q in range(per):
            part = jnp.zeros((span, LANES), jnp.float32)
            for r in range(width):
                part = jnp.where(wide == r, values[r * per + q][c * span : (c + 1) * span], part)
            parts.append(part)
        sbuf[me, c * width : (c + 1) * width, :] = jnp.concatenate(parts, axis=0).T[:width]

    def exchange(p):
        return pltpu.make_async_remote_copy(
            src_ref=sbuf.at[me], dst_ref=sbuf.at[me], send_sem=ss_sem.at[p], recv_sem=sr_sem.at[me],
            device_id=device(p), device_id_type=MESH,
        )

    def arrived(p):
        return pltpu.make_async_remote_copy(
            src_ref=sbuf.at[p], dst_ref=sbuf.at[p], send_sem=ss_sem.at[p], recv_sem=sr_sem.at[p],
            device_id=device(p), device_id_type=MESH,
        )

    @pl.loop(1, n)
    def _(i):
        exchange(lax.rem(me + i, n)).start()

    @pl.loop(1, n)
    def _(i):
        arrived(lax.rem(me + n - i, n)).wait_recv()

    def plane(c, i):
        x = sbuf[:, c * width + i // per, :]
        q = i % per
        return x if q == 0 else pltpu.roll(x, LANES - q * span, 1)

    own_row = lax.broadcasted_iota(jnp.int32, (n, LANES), 0) == me
    one_row = lax.broadcasted_iota(jnp.int32, (1, LANES), 1)
    square = lax.broadcasted_iota(jnp.int32, (LANES, LANES), 0)
    loss_here = jnp.zeros((1, 1), jnp.float32)
    columns = []
    for c in range(planes):
        at = [(plane(c, b), plane(c, here + b)) for b in range(here)]
        token_loss, grad_at, mass, norm = loss_planes(at, *(plane(c, 2 * here + i) for i in range(4)))
        mine = one_row + c * span == me
        loss_here = loss_here + jnp.sum(
            jnp.where(mine & (one_row < span), token_loss, 0.0), axis=1, keepdims=True
        )
        lines = [norm, mass] + [jnp.sum(jnp.where(own_row, x, 0.0), axis=0, keepdims=True) for x in grad_at]
        stacked = jnp.zeros((LANES, LANES), jnp.float32)
        for i, line in enumerate(lines):
            stacked = jnp.where(square == i, line, stacked)
        columns.append(stacked.T[:span])
    loss_ref[...] = loss_here
    column = jnp.concatenate(columns, axis=0)
    norm, mass = column[:, 0:1], column[:, 1:2]
    logit_grad = -mass * jnp.exp(student - norm)
    added = [jnp.where(hits[b], column[:, 2 + b : 3 + b], 0.0) for b in range(here)]
    logit_grad = (logit_grad + jnp.concatenate(added, axis=1)).astype(jnp.bfloat16)

    step = 2 * LANES
    for j in range(0, ws.shape[0], step):
        product = lax.dot_general(
            logit_grad, ws[j : j + step, :], (((1,), (1,)), ((), ())), preferred_element_type=jnp.float32
        )
        for h in range(step // LANES):
            c = j // LANES + h
            ps[c * n : (c + 1) * n, :] = product[:, h * LANES : (h + 1) * LANES]

    def scatter(p):
        return pltpu.make_async_remote_copy(
            src_ref=pbuf.at[p], dst_ref=rbuf.at[me], send_sem=ps_sem.at[p], recv_sem=pr_sem.at[me],
            device_id=device(p), device_id_type=MESH,
        )

    def gathered(p):
        return pltpu.make_async_remote_copy(
            src_ref=pbuf.at[p], dst_ref=rbuf.at[p], send_sem=ps_sem.at[p], recv_sem=pr_sem.at[p],
            device_id=device(p), device_id_type=MESH,
        )

    @pl.loop(1, n)
    def _(i):
        p = lax.rem(me + i, n)
        pbuf[p] = ps[pl.ds(p, ds_rows, stride=n), :].astype(jnp.bfloat16)
        scatter(p).start()

    own = ps[pl.ds(me, ds_rows, stride=n), :].astype(jnp.bfloat16).astype(jnp.float32)

    def collect(i, total):
        p = lax.rem(me + n - i, n)
        gathered(p).wait_recv()
        return total + rbuf[p].astype(jnp.float32)

    total = lax.fori_loop(1, n, collect, own)
    grad_ref[...] = total.astype(jnp.bfloat16)

    @pl.loop(1, V)
    def _(d):
        to_z(d).wait_send()

    @pl.loop(0, V)
    def _(a):
        for d in range(1, T):
            to_xy(a, d).wait_send()
        for b in range(T):
            to_core(a, b).wait_send()

    @pl.loop(1, n)
    def _(i):
        p = lax.rem(me + i, n)
        exchange(p).wait_send()
        scatter(p).wait_send()


def local(sizes, student_hidden, teacher_hidden, student_head, teacher_head, proposed_block, proposed_offset):
    V, T, S = sizes
    n = V * T * S
    ds, width = student_head.shape
    dt = teacher_head.shape[0]
    ds_rows, dt_rows = ds // LANES, dt // LANES
    rows = ds_rows + dt_rows + 8
    K = proposed_block.shape[1]
    values = 2 * (width // BLK) + 4
    dma = pltpu.SemaphoreType.DMA
    loss, grad = pl.pallas_call(
        functools.partial(kernel, sizes),
        out_shape=(
            jax.ShapeDtypeStruct((1, 1), jnp.float32),
            jax.ShapeDtypeStruct((ds_rows, LANES), jnp.bfloat16),
        ),
        in_specs=[pl.BlockSpec(memory_space=pl.ANY)] * 6,
        out_specs=(pl.BlockSpec(memory_space=pltpu.VMEM), pl.BlockSpec(memory_space=pltpu.VMEM)),
        scratch_shapes=[
            pltpu.VMEM((1, ds), jnp.bfloat16),
            pltpu.VMEM((1, dt), jnp.bfloat16),
            pltpu.VMEM((ds, width), jnp.bfloat16),
            pltpu.VMEM((dt, width), jnp.bfloat16),
            pltpu.VMEM((1, K), jnp.int32),
            pltpu.VMEM((1, K), jnp.int32),
            pltpu.VMEM((rows, LANES), jnp.float32),
            pltpu.VMEM((n, rows, LANES), jnp.bfloat16),
            pltpu.VMEM((rows * n, LANES), jnp.float32),
            pltpu.VMEM((n, values * n // LANES, LANES), jnp.float32),
            pltpu.VMEM((ds_rows * n, LANES), jnp.float32),
            pltpu.VMEM((n, ds_rows, LANES), jnp.bfloat16),
            pltpu.VMEM((n, ds_rows, LANES), jnp.bfloat16),
            dma((6,)),
            dma((V,)),
            dma((V, T)),
            dma((V, T)),
            dma((n,)),
            dma((n,)),
            dma((n,)),
            dma((n,)),
            dma((n,)),
        ],
        compiler_params=pltpu.CompilerParams(
            collective_id=0, has_side_effects=True, vmem_limit_bytes=48 * 1024 * 1024
        ),
        name="distill",
    )(student_hidden, teacher_hidden, student_head, teacher_head, proposed_block, proposed_offset)
    return loss.reshape((1,)), grad.reshape((1, ds))


def solution(mesh):
    row = P(("groups", "vocab", "tokens", "sub"), None)
    return jax.shard_map(
        functools.partial(local, tuple(mesh.shape[a] for a in AXES)),
        mesh=mesh,
        in_specs=(row, row, P(None, AXES), P(None, AXES), row, row),
        out_specs=(P(("groups", "vocab", "tokens", "sub")), row),
        check_vma=False,
    )
```

time: 327 us -> 38.6 us (0.12)
  blocking collectives: 261 us -> 0 us
  Pallas kernels: 0 us -> 29.2 us
  waiting for transfers between devices: 17.3 us -> 0 us
  local copies, waits for them, and re-layouts: 20.3 us -> 6.33 us
  between operations: 14.2 us -> 2.47 us
  other arithmetic: 9.01 us -> 0 us
  matrix products: 5.12 us -> 0 us
    all_gather x4 -> x0, blocking collectives: 157 us -> none  [the longest x1 43.3 us: local(): lax.all_gather(proposed_block, ('vocab', 'tokens', 'sub'), axis=0, tiled=...]
    psum x1 -> x0, blocking collectives: 42.9 us -> none  [local(): lax.psum((jnp.sum(jnp.exp(student_logits - student_peak[:, None]), axis=1...]
    pmax x1 -> x0, blocking collectives: 37 us -> none  [local(): lax.pmax((student_peak, teacher_peak), ('vocab', 'tokens', 'sub'))]
    pallas_call x0 -> x1, Pallas kernels: none -> 29.2 us  [local(): pl.pallas_call(functools.partial(kernel, sizes), out_shape=(jax.ShapeDtyp...]
    unnamed x1 -> x0, blocking collectives: 23.3 us -> none
    gather x5 -> x0, local copies, waits for them, and re-layouts: 17.4 us -> none  [the longest x3 8.73 us: local(): jnp.take_along_axis(student_logits, local_col, axis=1)]
    reduce_scatter x1 -> x0, waiting for transfers between devices: 17.3 us -> none  [local(): lax.psum_scatter(lax.dot_general(grad_narrow, student_head, (((1,), (1,))...]
    unnamed x5 -> x0, other arithmetic: 7.9 us -> none
  transfers between devices with their start and end apart: 1 -> 0, of which waited for: 1 -> 0; matrix products, arithmetic and copies ran while one was open for 0% -> 0% of each run, Pallas kernels for 0% -> 0%
where the time goes in v1:
time: 38.6 us; the launch traced here: 38 us
  Pallas kernels  29.2 us (76%)
  local copies, waits for them, and re-layouts  6.33 us (16%)
  between operations  2.47 us (6%)
    pallas_call x1, Pallas kernels, local(): pl.pallas_call(functools.partial(kernel, sizes), out_shape=(jax.ShapeDtyp...  29.2 us
    unnamed x13, local copies, waits for them, and re-layouts  6.33 us

profile of v1, /device:TPU:0, one launch (start us, length us, event | category | flops | bytes accessed | tf_op | source)
XLA Modules:
  0.0 38.0 jit_solution(14197935751128891132)
XLA Ops:
  0.6 0.0 copy-start
  0.6 1.6 %copy-done = bf16[4096,256]{1,0:T(8,128)(2,1)S(1)} copy-done((bf16[4096,256]{1,0:T(8,128)(2,1)S(1)}, bf16[4096,256]{1,0:T(8,128)(2,1)}, u32[]{:S(2)}) %copy-start) | copy-done | bytes 2097176
  2.2 0.0 copy-start.1
  2.2 1.4 %copy-done.1 = bf16[3072,256]{1,0:T(8,128)(2,1)S(1)} copy-done((bf16[3072,256]{1,0:T(8,128)(2,1)S(1)}, bf16[3072,256]{1,0:T(8,128)(2,1)}, u32[]{:S(2)}) %copy-start.1) | copy-done | bytes 1572888
  3.6 0.0 copy-start.2
  3.6 0.7 %copy-done.2 = bf16[1,4096]{1,0:T(2,128)(2,1)S(1)} copy-done((bf16[1,4096]{1,0:T(2,128)(2,1)S(1)}, bf16[1,4096]{1,0:T(2,128)(2,1)}, u32[]{:S(2)}) %copy-start.2) | copy-done | bytes 8216
  4.3 0.0 copy-start.3
  4.4 0.7 %copy-done.3 = bf16[1,3072]{1,0:T(2,128)(2,1)S(1)} copy-done((bf16[1,3072]{1,0:T(2,128)(2,1)S(1)}, bf16[1,3072]{1,0:T(2,128)(2,1)}, u32[]{:S(2)}) %copy-start.3) | copy-done | bytes 6168
  5.1 0.0 copy-start.4
  5.1 0.7 %copy-done.4 = s32[1,32]{1,0:T(1,128)S(1)} copy-done((s32[1,32]{1,0:T(1,128)S(1)}, s32[1,32]{1,0:T(1,128)}, u32[]{:S(2)}) %copy-start.4) | copy-done | bytes 152
  5.7 0.0 copy-start.5
  5.7 0.7 %copy-done.5 = s32[1,32]{1,0:T(1,128)S(1)} copy-done((s32[1,32]{1,0:T(1,128)S(1)}, s32[1,32]{1,0:T(1,128)}, u32[]{:S(2)}) %copy-start.5) | copy-done | bytes 152
  6.4 29.2 %distill.1 = (f32[1,1]{1,0:T(1,128)}, bf16[24,128]{1,0:T(8,128)(2,1)S(1)}) custom-call(bf16[1,3072]{1,0:T(2,128)(2,1)S(1)} %copy-done.3, bf16[1,4096]{1,0:T(2,128)(2,1)S(1)} %copy-done.2, bf16[3072,256]{1,0:T(8,128)(2,1)S(1)} %copy-done.1, bf16[4096,256]{1,0:T(8,128)(2,1)S(1)} %copy-done, s32[1,32]{1,0:T(1,128)S(1)} %copy-done.4, s32[1,32]{1,0:T(1,128)S(1)} %copy-done.5), custom_call_target="tpu_custom_call" | custom-call | tf_op jit(solution)/shard_map/distill/pallas_call | solution.py:315
  35.6 0.6 %copy.10 = bf16[1,1,24,128]{3,1,2,0:T(2,128)(2,1)} copy(bf16[1,1,24,128]{3,2,1,0:T(8,128)(2,1)S(1)} %bitcast.6) | data formatting | bytes 12288
Async XLA Ops:
  0.6 1.6 %copy-start = (bf16[4096,256]{1,0:T(8,128)(2,1)S(1)}, bf16[4096,256]{1,0:T(8,128)(2,1)}, u32[]{:S(2)}) copy-start(bf16[4096,256]{1,0:T(8,128)(2,1)} %wt_hbm.1) | copy-start | bytes 6291460
  2.2 1.4 %copy-start.1 = (bf16[3072,256]{1,0:T(8,128)(2,1)S(1)}, bf16[3072,256]{1,0:T(8,128)(2,1)}, u32[]{:S(2)}) copy-start(bf16[3072,256]{1,0:T(8,128)(2,1)} %ws_hbm.1) | copy-start | bytes 4718596
  3.6 0.7 %copy-start.2 = (bf16[1,4096]{1,0:T(2,128)(2,1)S(1)}, bf16[1,4096]{1,0:T(2,128)(2,1)}, u32[]{:S(2)}) copy-start(bf16[1,4096]{1,0:T(2,128)(2,1)} %th_hbm.1) | copy-start | bytes 24580
  4.3 0.7 %copy-start.3 = (bf16[1,3072]{1,0:T(2,128)(2,1)S(1)}, bf16[1,3072]{1,0:T(2,128)(2,1)}, u32[]{:S(2)}) copy-start(bf16[1,3072]{1,0:T(2,128)(2,1)} %sh_hbm.1) | copy-start | bytes 18436
  5.1 0.7 %copy-start.4 = (s32[1,32]{1,0:T(1,128)S(1)}, s32[1,32]{1,0:T(1,128)}, u32[]{:S(2)}) copy-start(s32[1,32]{1,0:T(1,128)} %blk_hbm.1) | copy-start | bytes 388
  5.7 0.7 %copy-start.5 = (s32[1,32]{1,0:T(1,128)S(1)}, s32[1,32]{1,0:T(1,128)}, u32[]{:S(2)}) copy-start(s32[1,32]{1,0:T(1,128)} %off_hbm.1) | copy-start | bytes 388

commit v2 on v1

--- a/solution.py
+++ b/solution.py
@@ -54,9 +54,6 @@
     ds_rows, dt_rows = sh.shape[1] // LANES, th.shape[1] // LANES
     rows = gbuf.shape[1]
 
-    def device(p):
-        return (g, p // (T * S), (p // S) % T, p % S)
-
     def slot(a, b, c):
         return (a * T + b) * S + c
 
@@ -69,11 +66,23 @@
     for load in loads:
         load.start()
 
+    def turn(x, size):
+        return jnp.where(x >= size, x - size, x)
+
     barrier = pltpu.get_barrier_semaphore()
-
-    @pl.loop(1, n)
-    def _(i):
-        pl.semaphore_signal(barrier, inc=1, device_id=device(lax.rem(me + i, n)), device_id_type=MESH)
+    other = turn(s + 1, S)
+    along = [turn(t + d, T) for d in range(T)]
+
+    def greet(to):
+        pl.semaphore_signal(barrier, inc=1, device_id=to, device_id_type=MESH)
+
+    @pl.loop(1, V)
+    def _(d):
+        greet((g, turn(v + d, V), t, s))
+
+    for d in range(1, T):
+        greet((g, v, along[d], s))
+    greet((g, v, t, other))
 
     for load in loads[:4]:
         load.wait()
@@ -91,7 +100,7 @@
     stage[base + 2 : base + 3, :K] = off[...].astype(jnp.float32)
     gbuf[me] = stage[...].astype(jnp.bfloat16)
 
-    pl.semaphore_wait(barrier, n - 1)
+    pl.semaphore_wait(barrier, V - 1 + T - 1 + 1)
 
     def send(at, to, sem):
         return pltpu.make_async_remote_copy(
@@ -99,13 +108,11 @@
             device_id=to, device_id_type=MESH,
         )
 
-    other = lax.rem(s + 1, S)
-
     def to_z(d):
-        return send(me, (g, lax.rem(v + d, V), t, s), gz_sem.at[d])
+        return send(me, (g, turn(v + d, V), t, s), gz_sem.at[d])
 
     def to_xy(a, d):
-        return send(slot(a, t, s), (g, v, lax.rem(t + d, T), s), gx_sem.at[a, d])
+        return send(slot(a, t, s), (g, v, along[d], s), gx_sem.at[a, d])
 
     def to_core(a, b):
         return send(slot(a, b, s), (g, v, t, other), gc_sem.at[a, b])
@@ -124,7 +131,7 @@
 
     @pl.loop(1, V)
     def _(d):
-        a = lax.rem(v + V - d, V)
+        a = turn(v + V - d, V)
         send(slot(a, t, s), (g, v, t, other), gc_sem.at[a, t]).wait_recv()
         for e in range(1, T):
             to_xy(a, e).start()
@@ -133,18 +140,18 @@
 
     @pl.loop(0, V)
     def _(d):
-        a = lax.rem(v + V - d, V)
+        a = turn(v + V - d, V)
         for e in range(1, T):
-            b = lax.rem(t + T - e, T)
+            b = along[(T - e) % T]
             to_core(a, b).wait_recv()
             to_core(a, b).start()
             unpack(slot(a, b, s))
 
     @pl.loop(0, V)
     def _(d):
-        a = lax.rem(v + V - d, V)
+        a = turn(v + V - d, V)
         for e in range(T):
-            b = lax.rem(t + T - e, T)
+            b = along[(T - e) % T]
             at = slot(a, b, other)
             send(at, (g, v, t, other), gc_sem.at[a, b]).wait_recv()
             unpack(at)
@@ -198,25 +205,36 @@
             parts.append(part)
         sbuf[me, c * width : (c + 1) * width, :] = jnp.concatenate(parts, axis=0).T[:width]
 
-    def exchange(p):
+    def everyone(act):
+        for d in range(1, T * S + 1):
+            b, c = along[d // S % T], (other if d % S else s)
+
+            @pl.loop(1 if d == T * S else 0, V)
+            def _(e):
+                a = turn(v + e, V)
+                act((g, a, b, c), slot(a, b, c))
+
+    def exchange(to):
         return pltpu.make_async_remote_copy(
-            src_ref=sbuf.at[me], dst_ref=sbuf.at[me], send_sem=ss_sem.at[p], recv_sem=sr_sem.at[me],
-            device_id=device(p), device_id_type=MESH,
-        )
-
-    def arrived(p):
+            src_ref=sbuf.at[me], dst_ref=sbuf.at[me], send_sem=ss_sem, recv_sem=sr_sem,
+            device_id=to, device_id_type=MESH,
+        )
+
+    def scatter(to, p):
         return pltpu.make_async_remote_copy(
-            src_ref=sbuf.at[p], dst_ref=sbuf.at[p], send_sem=ss_sem.at[p], recv_sem=sr_sem.at[p],
-            device_id=device(p), device_id_type=MESH,
-        )
-
-    @pl.loop(1, n)
-    def _(i):
-        exchange(lax.rem(me + i, n)).start()
-
-    @pl.loop(1, n)
-    def _(i):
-        arrived(lax.rem(me + n - i, n)).wait_recv()
+            src_ref=pbuf.at[p], dst_ref=rbuf.at[me], send_sem=ps_sem, recv_sem=pr_sem,
+            device_id=to, device_id_type=MESH,
+        )
+
+    def total_of(buf, send_sem, recv_sem):
+        part = buf.at[pl.ds(0, n - 1)]
+        return pltpu.make_async_remote_copy(
+            src_ref=part, dst_ref=part, send_sem=send_sem, recv_sem=recv_sem,
+            device_id=(g, v, t, other), device_id_type=MESH,
+        )
+
+    everyone(lambda to, p: exchange(to).start())
+    total_of(sbuf, ss_sem, sr_sem).wait_recv()
 
     def plane(c, i):
         x = sbuf[:, c * width + i // per, :]
@@ -256,33 +274,20 @@
             c = j // LANES + h
             ps[c * n : (c + 1) * n, :] = product[:, h * LANES : (h + 1) * LANES]
 
-    def scatter(p):
-        return pltpu.make_async_remote_copy(
-            src_ref=pbuf.at[p], dst_ref=rbuf.at[me], send_sem=ps_sem.at[p], recv_sem=pr_sem.at[me],
-            device_id=device(p), device_id_type=MESH,
-        )
-
-    def gathered(p):
-        return pltpu.make_async_remote_copy(
-            src_ref=pbuf.at[p], dst_ref=rbuf.at[p], send_sem=ps_sem.at[p], recv_sem=pr_sem.at[p],
-            device_id=device(p), device_id_type=MESH,
-        )
-
-    @pl.loop(1, n)
-    def _(i):
-        p = lax.rem(me + i, n)
+    def pack(to, p):
         pbuf[p] = ps[pl.ds(p, ds_rows, stride=n), :].astype(jnp.bfloat16)
-        scatter(p).start()
-
-    own = ps[pl.ds(me, ds_rows, stride=n), :].astype(jnp.bfloat16).astype(jnp.float32)
-
-    def collect(i, total):
-        p = lax.rem(me + n - i, n)
-        gathered(p).wait_recv()
+        scatter(to, p).start()
+
+    everyone(pack)
+    rbuf[me] = ps[pl.ds(me, ds_rows, stride=n), :].astype(jnp.bfloat16)
+    total_of(rbuf, ps_sem, pr_sem).wait_recv()
+
+    def collect(p, total):
         return total + rbuf[p].astype(jnp.float32)
 
-    total = lax.fori_loop(1, n, collect, own)
-    grad_ref[...] = total.astype(jnp.bfloat16)
+    grad_ref[...] = lax.fori_loop(
+        0, n, collect, jnp.zeros(grad_ref.shape, jnp.float32), unroll=8
+    ).astype(jnp.bfloat16)
 
     @pl.loop(1, V)
     def _(d):
@@ -295,11 +300,8 @@
         for b in range(T):
             to_core(a, b).wait_send()
 
-    @pl.loop(1, n)
-    def _(i):
-        p = lax.rem(me + i, n)
-        exchange(p).wait_send()
-        scatter(p).wait_send()
+    total_of(sbuf, ss_sem, sr_sem).wait_send()
+    total_of(rbuf, ps_sem, pr_sem).wait_send()
 
 
 def local(sizes, student_hidden, teacher_hidden, student_head, teacher_head, proposed_block, proposed_offset):
@@ -318,7 +320,7 @@
             jax.ShapeDtypeStruct((1, 1), jnp.float32),
             jax.ShapeDtypeStruct((ds_rows, LANES), jnp.bfloat16),
         ),
-        in_specs=[pl.BlockSpec(memory_space=pl.ANY)] * 6,
+        in_specs=[pl.BlockSpec(memory_space=pltpu.HBM)] * 6,
         out_specs=(pl.BlockSpec(memory_space=pltpu.VMEM), pl.BlockSpec(memory_space=pltpu.VMEM)),
         scratch_shapes=[
             pltpu.VMEM((1, ds), jnp.bfloat16),
@@ -339,13 +341,13 @@
             dma((V, T)),
             dma((V, T)),
             dma((n,)),
-            dma((n,)),
-            dma((n,)),
-            dma((n,)),
-            dma((n,)),
+            dma,
+            dma,
+            dma,
+            dma,
         ],
         compiler_params=pltpu.CompilerParams(
-            collective_id=0, has_side_effects=True, vmem_limit_bytes=48 * 1024 * 1024
+            collective_id=0, has_side_effects=True, vmem_limit_bytes=56 * 1024 * 1024
         ),
         name="distill",
     )(student_hidden, teacher_hidden, student_head, teacher_head, proposed_block, proposed_offset)

time: 38.6 us -> 32.2 us (0.83)
  local copies, waits for them, and re-layouts: 6.33 us -> 1.3 us
  Pallas kernels: 29.2 us -> 28.2 us
    unnamed x13 -> x1, local copies, waits for them, and re-layouts: 6.33 us -> 1.3 us
    pallas_call x1, Pallas kernels: 29.2 us -> 28.2 us  [local(): pl.pallas_call(functools.partial(kernel, sizes), out_shape=(jax.ShapeDtyp...]
where the time goes in v2:
time: 32.2 us; the launch traced here: 31.9 us
  Pallas kernels  28.2 us (88%)
  between operations  2.4 us (7%)
  local copies, waits for them, and re-layouts  1.3 us (4%)
    pallas_call x1, Pallas kernels, local(): pl.pallas_call(functools.partial(kernel, sizes), out_shape=(jax.ShapeDtyp...  28.2 us
    unnamed x1, local copies, waits for them, and re-layouts  1.3 us

profile of v2, /device:TPU:0, one launch (start us, length us, event | category | flops | bytes accessed | tf_op | source)
XLA Modules:
  0.0 31.9 jit_solution(1982737887716771435)
XLA Ops:
  0.6 28.2 %distill.1 = (f32[1,1]{1,0:T(1,128)}, bf16[24,128]{1,0:T(8,128)(2,1)}) custom-call(bf16[1,3072]{1,0:T(2,128)(2,1)} %sh_hbm.1, bf16[1,4096]{1,0:T(2,128)(2,1)} %th_hbm.1, bf16[3072,256]{1,0:T(8,128)(2,1)} %ws_hbm.1, bf16[4096,256]{1,0:T(8,128)(2,1)} %wt_hbm.1, s32[1,32]{1,0:T(1,128)} %blk_hbm.1, s32[1,32]{1,0:T(1,128)} %off_hbm.1), custom_call_target="tpu_custom_call" | custom-call | tf_op jit(solution)/shard_map/distill/pallas_call | solution.py:317
  28.9 1.3 %copy.10 = bf16[1,1,24,128]{3,1,2,0:T(2,128)(2,1)} copy(bf16[1,1,24,128]{3,2,1,0:T(8,128)(2,1)} %bitcast.7) | data formatting | bytes 12288

commit v3 on v2

--- a/solution.py
+++ b/solution.py
@@ -69,6 +69,22 @@
     def turn(x, size):
         return jnp.where(x >= size, x - size, x)
 
+    def outward(act, inward=False):
+        @pl.loop(1, V)
+        def _(d):
+            d = V - d if inward else d
+
+            @pl.when(v >= d)
+            def _():
+                act(v - d)
+
+            @pl.when(v + d < V)
+            def _():
+                act(v + d)
+
+    def inward(act):
+        outward(act, inward=True)
+
     barrier = pltpu.get_barrier_semaphore()
     other = turn(s + 1, S)
     along = [turn(t + d, T) for d in range(T)]
@@ -76,10 +92,7 @@
     def greet(to):
         pl.semaphore_signal(barrier, inc=1, device_id=to, device_id_type=MESH)
 
-    @pl.loop(1, V)
-    def _(d):
-        greet((g, turn(v + d, V), t, s))
-
+    inward(lambda a: greet((g, a, t, s)))
     for d in range(1, T):
         greet((g, v, along[d], s))
     greet((g, v, t, other))
@@ -108,8 +121,8 @@
             device_id=to, device_id_type=MESH,
         )
 
-    def to_z(d):
-        return send(me, (g, turn(v + d, V), t, s), gz_sem.at[d])
+    def to_z(a):
+        return send(me, (g, a, t, s), gz_sem.at[a])
 
     def to_xy(a, d):
         return send(slot(a, t, s), (g, v, along[d], s), gx_sem.at[a, d])
@@ -120,41 +133,35 @@
     def unpack(at):
         xs[pl.ds(at, rows, stride=n), :] = gbuf[at].astype(jnp.float32)
 
-    @pl.loop(1, V)
-    def _(d):
-        to_z(d).start()
-
+    inward(lambda a: to_z(a).start())
     for d in range(1, T):
         to_xy(v, d).start()
     to_core(v, t).start()
     unpack(me)
 
-    @pl.loop(1, V)
-    def _(d):
-        a = turn(v + V - d, V)
-        send(slot(a, t, s), (g, v, t, other), gc_sem.at[a, t]).wait_recv()
+    def from_z(a):
+        to_core(a, t).wait_recv()
         for e in range(1, T):
             to_xy(a, e).start()
         to_core(a, t).start()
         unpack(slot(a, t, s))
 
-    @pl.loop(0, V)
-    def _(d):
-        a = turn(v + V - d, V)
-        for e in range(1, T):
-            b = along[(T - e) % T]
+    def from_xy(a):
+        for b in along[1:]:
             to_core(a, b).wait_recv()
             to_core(a, b).start()
             unpack(slot(a, b, s))
 
-    @pl.loop(0, V)
-    def _(d):
-        a = turn(v + V - d, V)
-        for e in range(T):
-            b = along[(T - e) % T]
+    def from_core(a):
+        for b in along:
             at = slot(a, b, other)
             send(at, (g, v, t, other), gc_sem.at[a, b]).wait_recv()
             unpack(at)
+
+    outward(from_z)
+    for act in (from_xy, from_core):
+        act(v)
+        outward(act)
 
     def chunks(lo, hi):
         return jnp.concatenate([xs[c * n : (c + 1) * n, :] for c in range(lo, hi)], axis=1).astype(jnp.bfloat16)
@@ -206,13 +213,15 @@
         sbuf[me, c * width : (c + 1) * width, :] = jnp.concatenate(parts, axis=0).T[:width]
 
     def everyone(act):
-        for d in range(1, T * S + 1):
-            b, c = along[d // S % T], (other if d % S else s)
-
-            @pl.loop(1 if d == T * S else 0, V)
-            def _(e):
-                a = turn(v + e, V)
+        places = [(along[d], c) for d in range(T) for c in (s, other)]
+
+        def shard(a):
+            for b, c in places:
                 act((g, a, b, c), slot(a, b, c))
+
+        inward(shard)
+        for b, c in places[1:]:
+            act((g, v, b, c), slot(v, b, c))
 
     def exchange(to):
         return pltpu.make_async_remote_copy(
@@ -289,9 +298,7 @@
         0, n, collect, jnp.zeros(grad_ref.shape, jnp.float32), unroll=8
     ).astype(jnp.bfloat16)
 
-    @pl.loop(1, V)
-    def _(d):
-        to_z(d).wait_send()
+    outward(lambda a: to_z(a).wait_send())
 
     @pl.loop(0, V)
     def _(a):

time: 32.2 us -> 31.6 us (0.981)
  Pallas kernels: 28.2 us -> 27.6 us
    pallas_call x1, Pallas kernels: 28.2 us -> 27.6 us  [local(): pl.pallas_call(functools.partial(kernel, sizes), out_shape=(jax.ShapeDtyp...]
where the time goes in v3:
time: 31.6 us; the launch traced here: 31.3 us
  Pallas kernels  27.6 us (87%)
  between operations  2.4 us (8%)
  local copies, waits for them, and re-layouts  1.3 us (4%)
    pallas_call x1, Pallas kernels, local(): pl.pallas_call(functools.partial(kernel, sizes), out_shape=(jax.ShapeDtyp...  27.6 us
    unnamed x1, local copies, waits for them, and re-layouts  1.3 us

profile of v3, /device:TPU:0, one launch (start us, length us, event | category | flops | bytes accessed | tf_op | source)
XLA Modules:
  0.0 31.3 jit_solution(3616059236149364499)
XLA Ops:
  0.6 27.6 %distill.1 = (f32[1,1]{1,0:T(1,128)}, bf16[24,128]{1,0:T(8,128)(2,1)}) custom-call(bf16[1,3072]{1,0:T(2,128)(2,1)} %sh_hbm.1, bf16[1,4096]{1,0:T(2,128)(2,1)} %th_hbm.1, bf16[3072,256]{1,0:T(8,128)(2,1)} %ws_hbm.1, bf16[4096,256]{1,0:T(8,128)(2,1)} %wt_hbm.1, s32[1,32]{1,0:T(1,128)} %blk_hbm.1, s32[1,32]{1,0:T(1,128)} %off_hbm.1), custom_call_target="tpu_custom_call" | custom-call | tf_op jit(solution)/shard_map/distill/pallas_call | solution.py:324
  28.3 1.3 %copy.10 = bf16[1,1,24,128]{3,1,2,0:T(2,128)(2,1)} copy(bf16[1,1,24,128]{3,2,1,0:T(8,128)(2,1)} %bitcast.7) | data formatting | bytes 12288

commit v4 on v3

--- a/solution.py
+++ b/solution.py
@@ -42,7 +42,7 @@
 
 
 def kernel(
-    sizes, sh_hbm, th_hbm, ws_hbm, wt_hbm, blk_hbm, off_hbm, loss_ref, grad_ref,
+    sizes, sh_hbm, th_hbm, ws_hbm, wt_hbm, blk_hbm, off_hbm, out_ref,
     sh, th, ws, wt, blk, off, stage, gbuf, xs, sbuf, ps, pbuf, rbuf,
     load_sem, gz_sem, gx_sem, gc_sem, gr_sem, ss_sem, sr_sem, ps_sem, pr_sem,
 ):
@@ -267,7 +267,7 @@
         for i, line in enumerate(lines):
             stacked = jnp.where(square == i, line, stacked)
         columns.append(stacked.T[:span])
-    loss_ref[...] = loss_here
+    out_ref[ds_rows:, :] = jnp.broadcast_to(loss_here, (8, LANES))
     column = jnp.concatenate(columns, axis=0)
     norm, mass = column[:, 0:1], column[:, 1:2]
     logit_grad = -mass * jnp.exp(student - norm)
@@ -294,9 +294,9 @@
     def collect(p, total):
         return total + rbuf[p].astype(jnp.float32)
 
-    grad_ref[...] = lax.fori_loop(
-        0, n, collect, jnp.zeros(grad_ref.shape, jnp.float32), unroll=8
-    ).astype(jnp.bfloat16)
+    out_ref[:ds_rows, :] = lax.fori_loop(
+        0, n, collect, jnp.zeros((ds_rows, LANES), jnp.float32), unroll=8
+    )
 
     outward(lambda a: to_z(a).wait_send())
 
@@ -309,6 +309,13 @@
 
     total_of(sbuf, ss_sem, sr_sem).wait_send()
     total_of(rbuf, ps_sem, pr_sem).wait_send()
+
+
+def finish(out_ref, loss_ref, grad_ref):
+    ds_rows = out_ref.shape[0] - 8
+    for j in range(ds_rows):
+        grad_ref[:, j * LANES : (j + 1) * LANES] = out_ref[j : j + 1, :].astype(jnp.bfloat16)
+    loss_ref[...] = out_ref[ds_rows : ds_rows + 1, 0:1]
 
 
 def local(sizes, student_hidden, teacher_hidden, student_head, teacher_head, proposed_block, proposed_offset):
@@ -321,14 +328,11 @@
     K = proposed_block.shape[1]
     values = 2 * (width // BLK) + 4
     dma = pltpu.SemaphoreType.DMA
-    loss, grad = pl.pallas_call(
+    result = pl.pallas_call(
         functools.partial(kernel, sizes),
-        out_shape=(
-            jax.ShapeDtypeStruct((1, 1), jnp.float32),
-            jax.ShapeDtypeStruct((ds_rows, LANES), jnp.bfloat16),
-        ),
-        in_specs=[pl.BlockSpec(memory_space=pltpu.HBM)] * 6,
-        out_specs=(pl.BlockSpec(memory_space=pltpu.VMEM), pl.BlockSpec(memory_space=pltpu.VMEM)),
+        out_shape=jax.ShapeDtypeStruct((ds_rows + 8, LANES), jnp.float32),
+        in_specs=[pl.BlockSpec(memory_space=pl.ANY)] * 6,
+        out_specs=pl.BlockSpec(memory_space=pltpu.VMEM),
         scratch_shapes=[
             pltpu.VMEM((1, ds), jnp.bfloat16),
             pltpu.VMEM((1, dt), jnp.bfloat16),
@@ -358,7 +362,14 @@
         ),
         name="distill",
     )(student_hidden, teacher_hidden, student_head, teacher_head, proposed_block, proposed_offset)
-    return loss.reshape((1,)), grad.reshape((1, ds))
+    loss, grad = pl.pallas_call(
+        finish,
+        out_shape=(jax.ShapeDtypeStruct((1, 1), jnp.float32), jax.ShapeDtypeStruct((1, ds), jnp.bfloat16)),
+        in_specs=[pl.BlockSpec(memory_space=pltpu.VMEM)],
+        out_specs=(pl.BlockSpec(memory_space=pltpu.VMEM), pl.BlockSpec(memory_space=pltpu.VMEM)),
+        name="finish",
+    )(result)
+    return loss.reshape((1,)), grad
 
 
 def solution(mesh):

time: 31.6 us -> 29.9 us (0.946)
  between operations: 2.4 us -> 0.64 us
  Pallas kernels: 27.6 us -> 29 us
  local copies, waits for them, and re-layouts: 1.3 us -> 0 us
    pallas_call x1 -> x2, Pallas kernels: 27.6 us -> 29 us  [the longest x1 27.6 us: local(): pl.pallas_call(functools.partial(kernel, sizes), out_shape=jax.ShapeDtype...]
    unnamed x1 -> x0, local copies, waits for them, and re-layouts: 1.3 us -> none
where the time goes in v4:
time: 29.9 us; the launch traced here: 29.6 us
  Pallas kernels  29 us (97%)
  between operations  0.64 us (2%)
    pallas_call x1, Pallas kernels, local(): pl.pallas_call(functools.partial(kernel, sizes), out_shape=jax.ShapeDtype...  27.6 us
    pallas_call x1, Pallas kernels, local(): pl.pallas_call(finish, out_shape=(jax.ShapeDtypeStruct((1, 1), jnp.float3...  1.34 us

profile of v4, /device:TPU:0, one launch (start us, length us, event | category | flops | bytes accessed | tf_op | source)
XLA Modules:
  0.0 29.6 jit_solution(10753748248984225228)
XLA Ops:
  0.6 27.6 %distill.1.out_ref = f32[32,128]{1,0:T(8,128)} custom-call(bf16[1,3072]{1,0:T(2,128)(2,1)} %sh_hbm.1, bf16[1,4096]{1,0:T(2,128)(2,1)} %th_hbm.1, bf16[3072,256]{1,0:T(8,128)(2,1)} %ws_hbm.1, bf16[4096,256]{1,0:T(8,128)(2,1)} %wt_hbm.1, s32[1,32]{1,0:T(1,128)} %blk_hbm.1, s32[1,32]{1,0:T(1,128)} %off_hbm.1), custom_call_target="tpu_custom_call" | custom-call | tf_op jit(solution)/shard_map/distill/pallas_call | solution.py:331
  28.3 1.3 %finish.1 = (f32[1,1]{1,0:T(1,128)}, bf16[1,3072]{1,0:T(2,128)(2,1)}) custom-call(f32[32,128]{1,0:T(8,128)} %distill.1.out_ref), custom_call_target="tpu_custom_call" | custom-call | tf_op jit(solution)/shard_map/finish/pallas_call | solution.py:365

commit v5 on v4

--- a/solution.py
+++ b/solution.py
@@ -44,7 +44,7 @@
 def kernel(
     sizes, sh_hbm, th_hbm, ws_hbm, wt_hbm, blk_hbm, off_hbm, out_ref,
     sh, th, ws, wt, blk, off, stage, gbuf, xs, sbuf, ps, pbuf, rbuf,
-    load_sem, gz_sem, gx_sem, gc_sem, gr_sem, ss_sem, sr_sem, ps_sem, pr_sem,
+    load_sem, gz_sem, gx_sem, gc_sem, gr_sem, ss_sem, sr_sem, ps_sem, pr_sem, cs_sem, cr_sem,
 ):
     V, T, S = sizes
     n = V * T * S
@@ -229,21 +229,30 @@
             device_id=to, device_id_type=MESH,
         )
 
-    def scatter(to, p):
+    chips = V * T
+
+    def to_pair(a):
         return pltpu.make_async_remote_copy(
-            src_ref=pbuf.at[p], dst_ref=rbuf.at[me], send_sem=ps_sem, recv_sem=pr_sem,
-            device_id=to, device_id_type=MESH,
-        )
-
-    def total_of(buf, send_sem, recv_sem):
-        part = buf.at[pl.ds(0, n - 1)]
+            src_ref=pbuf.at[pl.ds(a * T, T)], dst_ref=rbuf.at[pl.ds(a * T, T)],
+            send_sem=cs_sem.at[a], recv_sem=cr_sem.at[a],
+            device_id=(g, v, t, other), device_id_type=MESH,
+        )
+
+    def scatter(a, b):
+        return pltpu.make_async_remote_copy(
+            src_ref=pbuf.at[chips + a * T + b], dst_ref=rbuf.at[chips + v * T + t], send_sem=ps_sem, recv_sem=pr_sem,
+            device_id=(g, a, b, s), device_id_type=MESH,
+        )
+
+    def total_of(buf, count, send_sem, recv_sem):
+        part = buf.at[pl.ds(0, count)]
         return pltpu.make_async_remote_copy(
             src_ref=part, dst_ref=part, send_sem=send_sem, recv_sem=recv_sem,
             device_id=(g, v, t, other), device_id_type=MESH,
         )
 
     everyone(lambda to, p: exchange(to).start())
-    total_of(sbuf, ss_sem, sr_sem).wait_recv()
+    total_of(sbuf, n - 1, ss_sem, sr_sem).wait_recv()
 
     def plane(c, i):
         x = sbuf[:, c * width + i // per, :]
@@ -283,19 +292,39 @@
             c = j // LANES + h
             ps[c * n : (c + 1) * n, :] = product[:, h * LANES : (h + 1) * LANES]
 
-    def pack(to, p):
-        pbuf[p] = ps[pl.ds(p, ds_rows, stride=n), :].astype(jnp.bfloat16)
-        scatter(to, p).start()
-
-    everyone(pack)
-    rbuf[me] = ps[pl.ds(me, ds_rows, stride=n), :].astype(jnp.bfloat16)
-    total_of(rbuf, ps_sem, pr_sem).wait_recv()
-
-    def collect(p, total):
-        return total + rbuf[p].astype(jnp.float32)
+    def partial(p):
+        return ps[pl.ds(p, ds_rows, stride=n), :].astype(jnp.bfloat16)
+
+    def give(a):
+        for b in range(T):
+            pbuf[a * T + b] = partial(slot(a, b, other))
+        to_pair(a).start()
+
+    inward(give)
+    give(v)
+
+    def paired(a, b):
+        return (partial(slot(a, b, s)).astype(jnp.float32) + rbuf[a * T + b].astype(jnp.float32)).astype(jnp.bfloat16)
+
+    def pack(a):
+        to_pair(a).wait_recv()
+        for b in along:
+            pbuf[chips + a * T + b] = paired(a, b)
+            scatter(a, b).start()
+
+    inward(pack)
+    to_pair(v).wait_recv()
+    for b in along[1:]:
+        pbuf[chips + v * T + b] = paired(v, b)
+        scatter(v, b).start()
+    rbuf[chips + v * T + t] = paired(v, t)
+    total_of(rbuf, chips - 1, ps_sem, pr_sem).wait_recv()
+
+    def collect(q, total):
+        return total + rbuf[chips + q].astype(jnp.float32)
 
     out_ref[:ds_rows, :] = lax.fori_loop(
-        0, n, collect, jnp.zeros((ds_rows, LANES), jnp.float32), unroll=8
+        0, chips, collect, jnp.zeros((ds_rows, LANES), jnp.float32), unroll=8
     )
 
     outward(lambda a: to_z(a).wait_send())
@@ -307,8 +336,13 @@
         for b in range(T):
             to_core(a, b).wait_send()
 
-    total_of(sbuf, ss_sem, sr_sem).wait_send()
-    total_of(rbuf, ps_sem, pr_sem).wait_send()
+    total_of(sbuf, n - 1, ss_sem, sr_sem).wait_send()
+
+    @pl.loop(0, V)
+    def _(a):
+        to_pair(a).wait_send()
+
+    total_of(rbuf, chips - 1, ps_sem, pr_sem).wait_send()
 
 
 def finish(out_ref, loss_ref, grad_ref):
@@ -356,6 +390,8 @@
             dma,
             dma,
             dma,
+            dma((V,)),
+            dma((V,)),
         ],
         compiler_params=pltpu.CompilerParams(
             collective_id=0, has_side_effects=True, vmem_limit_bytes=56 * 1024 * 1024
@@ -367,6 +403,7 @@
         out_shape=(jax.ShapeDtypeStruct((1, 1), jnp.float32), jax.ShapeDtypeStruct((1, ds), jnp.bfloat16)),
         in_specs=[pl.BlockSpec(memory_space=pltpu.VMEM)],
         out_specs=(pl.BlockSpec(memory_space=pltpu.VMEM), pl.BlockSpec(memory_space=pltpu.VMEM)),
+        compiler_params=pltpu.CompilerParams(vmem_limit_bytes=56 * 1024 * 1024),
         name="finish",
     )(result)
     return loss.reshape((1,)), grad

time: 29.9 us -> 29.6 us (0.990)
  Pallas kernels: 29 us -> 28.7 us
where the time goes in v5:
time: 29.6 us; the launch traced here: 29.3 us
  Pallas kernels  28.7 us (97%)
  between operations  0.64 us (2%)
    pallas_call x1, Pallas kernels, local(): pl.pallas_call(functools.partial(kernel, sizes), out_shape=jax.ShapeDtype...  27.4 us
    pallas_call x1, Pallas kernels, local(): pl.pallas_call(finish, out_shape=(jax.ShapeDtypeStruct((1, 1), jnp.float3...  1.34 us

profile of v5, /device:TPU:0, one launch (start us, length us, event | category | flops | bytes accessed | tf_op | source)
XLA Modules:
  0.0 29.3 jit_solution(7145519433954661468)
XLA Ops:
  0.6 27.4 %distill.1.out_ref = f32[32,128]{1,0:T(8,128)} custom-call(bf16[1,3072]{1,0:T(2,128)(2,1)} %sh_hbm.1, bf16[1,4096]{1,0:T(2,128)(2,1)} %th_hbm.1, bf16[3072,256]{1,0:T(8,128)(2,1)} %ws_hbm.1, bf16[4096,256]{1,0:T(8,128)(2,1)} %wt_hbm.1, s32[1,32]{1,0:T(1,128)} %blk_hbm.1, s32[1,32]{1,0:T(1,128)} %off_hbm.1), custom_call_target="tpu_custom_call" | custom-call | tf_op jit(solution)/shard_map/distill/pallas_call | solution.py:365
  28.0 1.3 %finish.1 = (f32[1,1]{1,0:T(1,128)}, bf16[1,3072]{1,0:T(2,128)(2,1)}) custom-call(f32[32,128]{1,0:T(8,128)} %distill.1.out_ref), custom_call_target="tpu_custom_call" | custom-call | tf_op jit(solution)/shard_map/finish/pallas_call | solution.py:401

commit v6 on v5

--- a/solution.py
+++ b/solution.py
@@ -376,9 +376,9 @@
             pltpu.VMEM((1, K), jnp.int32),
             pltpu.VMEM((rows, LANES), jnp.float32),
             pltpu.VMEM((n, rows, LANES), jnp.bfloat16),
-            pltpu.VMEM((rows * n, LANES), jnp.float32),
+            pltpu.VMEM(((rows + 1) * n, LANES), jnp.float32),
             pltpu.VMEM((n, values * n // LANES, LANES), jnp.float32),
-            pltpu.VMEM((ds_rows * n, LANES), jnp.float32),
+            pltpu.VMEM(((ds_rows + 1) * n, LANES), jnp.float32),
             pltpu.VMEM((n, ds_rows, LANES), jnp.bfloat16),
             pltpu.VMEM((n, ds_rows, LANES), jnp.bfloat16),
             dma((6,)),

time: 29.6 us -> 29.6 us (level)
  no operation moved by 1% of the time
where the time goes in v6:
time: 29.6 us; the launch traced here: 29.3 us
  Pallas kernels  28.7 us (97%)
  between operations  0.64 us (2%)
    pallas_call x1, Pallas kernels, local(): pl.pallas_call(functools.partial(kernel, sizes), out_shape=jax.ShapeDtype...  27.4 us
    pallas_call x1, Pallas kernels, local(): pl.pallas_call(finish, out_shape=(jax.ShapeDtypeStruct((1, 1), jnp.float3...  1.34 us

profile of v6, /device:TPU:0, one launch (start us, length us, event | category | flops | bytes accessed | tf_op | source)
XLA Modules:
  0.0 29.3 jit_solution(8213763533855902383)
XLA Ops:
  0.6 27.4 %distill.1.out_ref = f32[32,128]{1,0:T(8,128)} custom-call(bf16[1,3072]{1,0:T(2,128)(2,1)} %sh_hbm.1, bf16[1,4096]{1,0:T(2,128)(2,1)} %th_hbm.1, bf16[3072,256]{1,0:T(8,128)(2,1)} %ws_hbm.1, bf16[4096,256]{1,0:T(8,128)(2,1)} %wt_hbm.1, s32[1,32]{1,0:T(1,128)} %blk_hbm.1, s32[1,32]{1,0:T(1,128)} %off_hbm.1), custom_call_target="tpu_custom_call" | custom-call | tf_op jit(solution)/shard_map/distill/pallas_call | solution.py:365
  28.0 1.3 %finish.1 = (f32[1,1]{1,0:T(1,128)}, bf16[1,3072]{1,0:T(2,128)(2,1)}) custom-call(f32[32,128]{1,0:T(8,128)} %distill.1.out_ref), custom_call_target="tpu_custom_call" | custom-call | tf_op jit(solution)/shard_map/finish/pallas_call | solution.py:401
